TPU v7x, 32 devices: a whole 2x2x4 slice. The times are simulated.
32 devices in a mesh: comp: 8 (over z, y), lat: 4 (over x, core).
Axes of the slice: x: 2, y: 2, z: 4, core: 2. Of those that a mesh axis runs over, the one named last changes fastest.
Arguments:
- spectrum: float32 [32, 36, 384, 512], P('comp', None, 'lat'), may hold values from 0.1 to 3
- sea_mask: int32 [384, 512], P('lat'), may hold values from 0 to 1, as said below
- point_index: int32 [4, 32768], P('lat'), may hold values from 0 to 49151, as said below
- band_counts: int32 [4], P('lat'), may hold values from 16384 to 32768, as said below
- sub_counts: int32 [32], P('comp'), may hold values from 2 to 4, as said below
- mix_in: bfloat16 [1152, 1152], replicated, may hold values from -0.1875 to 0.1875
- mix_out: bfloat16 [1152, 1152], replicated, may hold values from -0.1875 to 0.1875
- growth: float32 [32, 36], replicated, may hold values from 0.05 to 1
- damping: float32 [32, 36], replicated, may hold values from 0.1 to 2
Outputs:
- new_spectrum: float32 [32, 36, 384, 512], P('comp', None, 'lat')
Inputs may be any that keep to these rules, and one draw needn't show every extreme that they name: `sea_mask`: exactly band_counts[b] of the 49152 cells of band b are sea. `point_index`: row b lists the sea cells of band b in increasing order in its first band_counts[b] slots, zeros after them. `band_counts`: some band has exactly 32768 sea cells. `sub_counts`: some frequency has exactly 4 substeps.
All inputs are finite; a program needn't handle non-finite values.
Results may differ from a plain program's by a relative error of at most 0.0015.
Values may be sent and summed in bfloat16 or wider, within the bound.
No kernel may reach another device: no remote copies, remote signals or barrier semaphores. Data moves between devices by JAX's collectives and lax.ppermute only.
A program may use at most 192 MiB of HBM per device.

v0:
```python
import functools

import jax
import jax.numpy as jnp
import numpy as np
from jax import lax
from jax.experimental import pallas as pl
from jax.experimental.pallas import tpu as pltpu
from jax.sharding import PartitionSpec as P

NSUB = 4
SUBLANES = 8
LANES = 128
BLOCK = 256
VMEM_BYTES = 56 * 1024 * 1024


def chunk_sizes(comp_count, shares):
    if comp_count % 16:
        return [comp_count]
    units, total = comp_count // 16, sum(shares)
    bounds = [units * sum(shares[:j]) // total for j in range(len(shares) + 1)]
    return [16 * (high - low) for low, high in zip(bounds, bounds[1:]) if high > low]


def wave_speeds(freq_index, sub_steps):
    group_speed = 1.4 * jnp.power(0.93, freq_index.astype(jnp.float32))
    return group_speed / sub_steps.astype(jnp.float32)


def direction_table(dir_count):
    angles = (np.arange(dir_count, dtype=np.float32) + np.float32(0.5)) * np.float32(
        2.0 * np.pi / dir_count
    )
    return [part(angles.astype(np.float64)).astype(np.float32) for part in (np.cos, np.sin)]


def freq_weights(freq_count, dir_count):
    raw_weight = jnp.power(1.1, jnp.arange(freq_count, dtype=jnp.float32))
    raw_weight = raw_weight / (dir_count * jnp.sum(raw_weight))
    return jnp.repeat(raw_weight, dir_count)


def propagate_kernel(
    start,
    speed_ref, steps_ref, cos_ref, sin_ref,
    spec_ref, low_ref, high_ref, mask_ref,
    *refs,
):
    out_ref, keep, even, odd = refs[-4:]
    block, rows, cols = spec_ref.shape
    halo = low_ref.shape[1]
    strips = rows // SUBLANES + 2
    parts = cols // LANES
    row_id = lax.broadcasted_iota(jnp.int32, (SUBLANES, LANES), 0)
    col_id = lax.broadcasted_iota(jnp.int32, (SUBLANES, LANES), 1)

    def strip_rows(s):
        return pl.ds(s * SUBLANES, SUBLANES)

    def run(i, ax, ay, steps, x_up, y_up):
        blank = jnp.zeros((SUBLANES - halo, cols), jnp.float32)
        for s in range(strips):
            keep[strip_rows(s), :] = (
                1.0
                - ax * mask_ref[2 if x_up else 1, strip_rows(s), :]
                - ay * mask_ref[4 if y_up else 3, strip_rows(s), :]
            )
            if s == 0:
                value = jnp.concatenate([blank, low_ref[i]], axis=0)
            elif s == strips - 1:
                value = jnp.concatenate([high_ref[i], blank], axis=0)
            else:
                value = spec_ref[i, strip_rows(s - 1), :]
            even[strip_rows(s), :] = value * mask_ref[0, strip_rows(s), :]

        edge_row = row_id == (0 if y_up else SUBLANES - 1)
        edge_col = col_id == (0 if x_up else LANES - 1)
        nothing = jnp.zeros((SUBLANES, LANES), jnp.float32)

        def substep(source, target):
            before_y = [nothing] * parts
            for s in range(strips) if y_up else range(strips - 1, -1, -1):
                before_x = nothing
                for t in range(parts) if x_up else range(parts - 1, -1, -1):
                    at = (strip_rows(s), slice(t * LANES, (t + 1) * LANES))
                    value = source[at]
                    turned = pltpu.roll(value, 1 if y_up else SUBLANES - 1, 0)
                    upwind_y = jnp.where(edge_row, before_y[t], turned)
                    before_y[t] = turned
                    turned = pltpu.roll(value, 1 if x_up else LANES - 1, 1)
                    upwind_x = jnp.where(edge_col, before_x, turned)
                    before_x = turned
                    target[at] = value * keep[at] + mask_ref[(0, *at)] * (
                        ax * upwind_x + ay * upwind_y
                    )

        def pair(_, carry):
            substep(even, odd)
            substep(odd, even)
            return carry

        lax.fori_loop(0, steps // 2, pair, 0)

        @pl.when(lax.rem(steps, 2) == 1)
        def _():
            substep(even, odd)
            out_ref[i] = odd[pl.ds(SUBLANES, rows), :]

        @pl.when(lax.rem(steps, 2) == 0)
        def _():
            out_ref[i] = even[pl.ds(SUBLANES, rows), :]

    def component(i, carry):
        at = start + pl.program_id(0) * block + i
        freq = at // cos_ref.shape[0]
        toward = at - freq * cos_ref.shape[0]
        cx, cy = speed_ref[freq] * cos_ref[toward], speed_ref[freq] * sin_ref[toward]
        steps = steps_ref[freq]
        for x_up in (True, False):
            for y_up in (True, False):

                @pl.when(((cx >= 0.0) == x_up) & ((cy >= 0.0) == y_up))
                def _():
                    run(i, cx if x_up else -cx, cy if y_up else -cy, steps, x_up, y_up)

        return carry

    lax.fori_loop(0, block, component, 0)


def propagate(scalars, spectrum, low, high, masks, start, size, low_start, chain):
    comp_count, rows, cols = spectrum.shape
    halo = low.shape[1]
    block = next(
        n for n in range(min(16, size), 0, -1)
        if size % n == 0 and start % n == 0 and low_start % n == 0
    )
    ext = masks.shape[1]
    cells = size * rows * cols
    return pl.pallas_call(
        functools.partial(propagate_kernel, start),
        grid_spec=pltpu.PrefetchScalarGridSpec(
            num_scalar_prefetch=4,
            grid=(size // block,),
            in_specs=[
                pl.BlockSpec((block, rows, cols), lambda g, *_: (start // block + g, 0, 0)),
                pl.BlockSpec((block, halo, cols), lambda g, *_: (low_start // block + g, 0, 0)),
                pl.BlockSpec((block, halo, cols), lambda g, *_: (low_start // block + g, 0, 0)),
                pl.BlockSpec(masks.shape, lambda g, *_: (0, 0, 0)),
            ]
            + [pl.BlockSpec(memory_space=pl.ANY) for _ in chain],
            out_specs=pl.BlockSpec((block, rows, cols), lambda g, *_: (start // block + g, 0, 0)),
            scratch_shapes=[pltpu.VMEM((ext, cols), jnp.float32) for _ in range(3)],
        ),
        out_shape=jax.ShapeDtypeStruct((comp_count, rows, cols), jnp.float32),
        input_output_aliases={8: 0} if chain else {},
        compiler_params=pltpu.CompilerParams(vmem_limit_bytes=VMEM_BYTES),
        cost_estimate=pl.CostEstimate(
            flops=cells * 30, bytes_accessed=cells * 8, transcendentals=0
        ),
        name="propagate",
    )(*scalars, spectrum, low, high, masks, *chain)


def selection(dest_row):
    slot = lax.broadcasted_iota(jnp.int32, (BLOCK, BLOCK), 0)
    slot = slot.astype(jnp.float32).astype(jnp.bfloat16)
    one, zero = jnp.ones((), jnp.bfloat16), jnp.zeros((), jnp.bfloat16)
    return jnp.where(slot == dest_row.astype(jnp.float32).astype(jnp.bfloat16), one, zero)


def tile_of(offset):
    return lax.shift_right_logical(offset, BLOCK.bit_length() - 1)


def lane_of(offset):
    return jnp.bitwise_and(offset, BLOCK - 1)


def tile_place(tile, per_group):
    lane = lax.rem(tile, per_group) * BLOCK
    return tile // per_group, slice(None), pl.ds(pl.multiple_of(lane, BLOCK), BLOCK)


def gather_kernel(offset_ref, field_ref, dest_ref, *refs):
    outs, (packed, rows_of, open_tile) = refs[:-3], refs[-3:]
    size, rows, cols = field_ref.shape
    blocks = cols // BLOCK
    per_group = packed.shape[2] // BLOCK
    step = pl.program_id(0)
    first_block = step * rows * blocks

    @pl.when(step == 0)
    def _():
        packed[...] = jnp.zeros_like(packed)
        open_tile[...] = jnp.zeros_like(open_tile)

    for t in range(cols // LANES):
        rows_of[t] = field_ref[:, :, t * LANES:(t + 1) * LANES].reshape(size * rows, LANES)

    lane_id = lax.broadcasted_iota(jnp.int32, (size, BLOCK), 1)
    begun = open_tile[...]
    for b in range(rows * blocks):
        r, t = b // blocks, b % blocks * (BLOCK // LANES)
        values = jnp.concatenate(
            [rows_of[t + i, pl.ds(r, size, stride=rows), :] for i in range(BLOCK // LANES)], axis=1
        ).astype(jnp.bfloat16)
        placed = lax.dot_general(
            values, selection(dest_ref[pl.ds(b, 1), :]), (((1,), (1,)), ((), ())),
            preferred_element_type=jnp.float32,
        )
        offset, following = offset_ref[first_block + b], offset_ref[first_block + b + 1]
        full = jnp.where(lane_id >= lane_of(offset), placed, begun)
        packed[tile_place(tile_of(offset), per_group)] = full.astype(jnp.bfloat16)
        begun = jnp.where(tile_of(following) > tile_of(offset), placed, full)
    open_tile[...] = begun

    @pl.when(step == pl.num_programs(0) - 1)
    def _():
        tile = tile_of(offset_ref[first_block + rows * blocks])
        packed[tile_place(tile, per_group)] = begun.astype(jnp.bfloat16)
        groups, _, width = outs[0].shape
        for h, out in enumerate(outs):
            out[...] = packed[:groups, :, h * width:(h + 1) * width]


def gather_points(offsets, dest, field, start, size, groups, per_group, pieces):
    rows, cols = field.shape[1:]
    parts = cols // LANES
    width = per_group // pieces
    return pl.pallas_call(
        gather_kernel,
        grid_spec=pltpu.PrefetchScalarGridSpec(
            num_scalar_prefetch=1,
            grid=(rows // SUBLANES,),
            in_specs=[
                pl.BlockSpec(
                    (pl.Element(size), pl.Element(SUBLANES), pl.Element(cols)),
                    lambda g, *_: (start, g * SUBLANES, 0),
                ),
                pl.BlockSpec((SUBLANES * cols // BLOCK, BLOCK), lambda g, *_: (g, 0)),
            ],
            out_specs=[
                pl.BlockSpec((groups, size, width), lambda g, *_: (0, 0, 0))
                for _ in range(pieces)
            ],
            scratch_shapes=[
                pltpu.VMEM((groups + 1, size, per_group), jnp.bfloat16),
                pltpu.VMEM((parts, size * SUBLANES, LANES), jnp.float32),
                pltpu.VMEM((size, BLOCK), jnp.float32),
            ],
        ),
        out_shape=[
            jax.ShapeDtypeStruct((groups, size, width), jnp.bfloat16) for _ in range(pieces)
        ],
        compiler_params=pltpu.CompilerParams(vmem_limit_bytes=VMEM_BYTES),
        cost_estimate=pl.CostEstimate(
            flops=size * rows * cols * 2 * BLOCK,
            bytes_accessed=size * rows * cols * 6,
            transcendentals=0,
        ),
        name="gather_points",
    )(offsets, field, dest)


def scatter_kernel(offset_ref, field_ref, dest_ref, first_ref, second_ref, *refs):
    out_ref, packed, rows_of = refs[-3:]
    size, rows, cols = field_ref.shape
    blocks = cols // BLOCK
    width = first_ref.shape[2]
    per_group = packed.shape[2] // BLOCK
    last_tile = packed.shape[0] * per_group - 1
    first_block = pl.program_id(0) * rows * blocks

    @pl.when(pl.program_id(0) == 0)
    def _():
        packed[:, :, :width] = first_ref[...]
        packed[:, :, width:] = second_ref[...]

    lane_id = lax.broadcasted_iota(jnp.int32, (size, BLOCK), 1)
    lane_id = lane_id.astype(jnp.float32).astype(jnp.bfloat16)
    for b in range(rows * blocks):
        r, t = b // blocks, b % blocks * (BLOCK // LANES)
        offset = offset_ref[first_block + b]
        tile = jnp.minimum(tile_of(offset), last_tile)
        following = jnp.minimum(tile + 1, last_tile)
        values = jnp.where(
            lane_id >= lane_of(offset).astype(jnp.float32).astype(jnp.bfloat16),
            packed[tile_place(tile, per_group)],
            packed[tile_place(following, per_group)],
        )
        found = jnp.dot(
            values, selection(dest_ref[pl.ds(b, 1), :]), preferred_element_type=jnp.float32
        )
        for i in range(BLOCK // LANES):
            rows_of[t + i, pl.ds(r, size, stride=rows), :] = found[:, i * LANES:(i + 1) * LANES]
    for t in range(cols // LANES):
        at = (slice(None), slice(None), slice(t * LANES, (t + 1) * LANES))
        out_ref[at] = field_ref[at] + rows_of[t].reshape(size, rows, LANES)


def scatter_points(offsets, dest, field, first, second, start):
    groups, size, width = second.shape
    rows, cols = field.shape[1:]
    parts = cols // LANES
    field_spec = pl.BlockSpec(
        (pl.Element(size), pl.Element(SUBLANES), pl.Element(cols)),
        lambda g, *_: (start, g * SUBLANES, 0),
    )
    return pl.pallas_call(
        scatter_kernel,
        grid_spec=pltpu.PrefetchScalarGridSpec(
            num_scalar_prefetch=1,
            grid=(rows // SUBLANES,),
            in_specs=[
                field_spec,
                pl.BlockSpec((SUBLANES * cols // BLOCK, BLOCK), lambda g, *_: (g, 0)),
                pl.BlockSpec(
                    (pl.Element(groups), pl.Element(size), pl.Element(width)),
                    lambda g, *_: (0, start, 0),
                ),
                pl.BlockSpec((groups, size, width), lambda g, *_: (0, 0, 0)),
            ],
            out_specs=field_spec,
            scratch_shapes=[
                pltpu.VMEM((groups, size, 2 * width), jnp.bfloat16),
                pltpu.VMEM((parts, size * SUBLANES, LANES), jnp.float32),
            ],
        ),
        out_shape=jax.ShapeDtypeStruct(field.shape, jnp.float32),
        input_output_aliases={1: 0},
        compiler_params=pltpu.CompilerParams(vmem_limit_bytes=VMEM_BYTES),
        cost_estimate=pl.CostEstimate(
            flops=size * rows * cols * 2 * BLOCK,
            bytes_accessed=size * rows * cols * 10,
            transcendentals=0,
        ),
        name="scatter_points",
    )(offsets, field, dest, first, second)


def source_kernel(counts, out_counts, groups, mix_in, mix_out, growth, damping, weight, *refs):
    ins, outs, points = refs[:len(counts)], refs[len(counts):-1], refs[-1]
    total = sum(counts)
    for g in range(groups):
        at = g * total
        for ref, count in zip(ins, counts):
            points[at:at + count, :] = ref[g * count:(g + 1) * count, :]
            at += count
    rounded = points[...]
    hidden = jnp.dot(mix_in[...], rounded, preferred_element_type=jnp.float32)
    square = (hidden * hidden).astype(jnp.bfloat16)
    transfer = jnp.dot(mix_out[...], square, preferred_element_type=jnp.float32)
    energy = rounded.astype(jnp.float32)
    mean_energy = jnp.sum(weight[...] * energy, axis=0, keepdims=True)
    increment = 0.5 * (
        growth[...] * energy
        + 0.25 * transfer
        - damping[...] * energy * (mean_energy / (1.0 + mean_energy))
    )
    increment = increment.astype(jnp.bfloat16)
    for g in range(groups):
        at = g * total
        for ref, count in zip(outs, out_counts):
            ref[g * count:(g + 1) * count, :] = increment[at:at + count, :]
            at += count


def source_terms(pieces, counts, out_counts, slots, starts, groups, mix_in, mix_out, columns):
    comp_count = mix_in.shape[0]
    width = min(512, slots)
    fixed = lambda g: (0, 0)
    if len(counts) == 1:
        counts, out_counts, groups = [comp_count], [comp_count], 1

    def moving(start):
        return lambda g: (0, start // width + g)

    return pl.pallas_call(
        functools.partial(source_kernel, counts, out_counts, groups),
        grid=(slots // width,),
        in_specs=[pl.BlockSpec(mix_in.shape, fixed)] * 2
        + [pl.BlockSpec((comp_count, 1), fixed)] * 3
        + [
            pl.BlockSpec((groups * count, width), moving(start))
            for count, start in zip(counts, starts)
        ],
        out_specs=[pl.BlockSpec((groups * count, width), moving(0)) for count in out_counts],
        out_shape=[
            jax.ShapeDtypeStruct((groups * count, slots), jnp.bfloat16) for count in out_counts
        ],
        scratch_shapes=[pltpu.VMEM((comp_count, width), jnp.bfloat16)],
        compiler_params=pltpu.CompilerParams(vmem_limit_bytes=VMEM_BYTES),
        cost_estimate=pl.CostEstimate(
            flops=4 * comp_count * comp_count * slots,
            bytes_accessed=4 * comp_count * (comp_count + slots),
            transcendentals=0,
        ),
        name="source_terms",
    )(mix_in, mix_out, *columns, *pieces)


def edge_rows(make, axis):
    count = lax.axis_size(axis)
    forward = [(i, i + 1) for i in range(count - 1)]
    backward = [(target, source) for source, target in forward]
    return lax.ppermute(make(True), axis, forward), lax.ppermute(make(False), axis, backward)


def mask_planes(sea_mask, low, high, strip):
    blank = jnp.zeros((strip - low.shape[0], sea_mask.shape[1]), jnp.float32)
    inner = sea_mask.astype(jnp.float32)
    mask = jnp.concatenate([blank, low, inner, high, blank], axis=0)
    row = jnp.zeros_like(mask[:1])
    col = jnp.zeros_like(mask[:, :1])
    left = jnp.concatenate([col, mask[:, :-1]], axis=1)
    right = jnp.concatenate([mask[:, 1:], col], axis=1)
    above = jnp.concatenate([row, mask[:-1]], axis=0)
    below = jnp.concatenate([mask[1:], row], axis=0)
    return jnp.stack([mask, left, right, above, below])


def slot_table(sea_mask):
    cells = sea_mask.reshape(-1, BLOCK).astype(jnp.float32)
    upto = jnp.triu(jnp.ones((BLOCK, BLOCK), jnp.float32))
    rank = jnp.dot(cells, upto, precision=lax.Precision.HIGHEST)
    count = rank[:, -1]
    blocks = cells.shape[0]
    before = jnp.tril(jnp.ones((blocks, blocks), jnp.float32), -1)
    offset = jnp.dot(before, count, precision=lax.Precision.HIGHEST)
    offset = jnp.append(offset, offset[-1] + count[-1]).astype(jnp.int32)
    place = lane_of(rank.astype(jnp.int32) - 1 + offset[:-1, None])
    return offset, jnp.where(cells > 0.0, place, -1)


def local(
    spectrum, sea_mask, point_index, band_counts, sub_counts, mix_in, mix_out, growth, damping
):
    freq_count, dir_count, row_count, lon_count = spectrum.shape
    comp_count = freq_count * dir_count
    all_count = growth.shape[0] * growth.shape[1]
    groups = lax.axis_size("comp")
    per_group = point_index.shape[1] // groups
    half = per_group // 2
    sizes = chunk_sizes(comp_count, (2, 3, 4))
    starts = [sum(sizes[:j]) for j in range(len(sizes))]
    out_sizes = chunk_sizes(comp_count, (7, 2))
    out_starts = [sum(out_sizes[:j]) for j in range(len(out_sizes))]

    field = spectrum.reshape(comp_count, row_count, lon_count)

    def first_edge(last):
        at = slice(row_count - NSUB, row_count) if last else slice(0, NSUB)
        mask_rows = sea_mask[at].astype(jnp.float32)
        return jnp.concatenate([field[:sizes[0], at], mask_rows[None]], axis=0)

    def later_edge(last):
        at = slice(row_count - NSUB, row_count) if last else slice(0, NSUB)
        return field[sizes[0]:, at]

    edges = [edge_rows(first_edge, "lat")]
    if len(sizes) > 1:
        edges.append(edge_rows(later_edge, "lat"))
    mask_low, mask_high = edges[0][0][sizes[0]], edges[0][1][sizes[0]]

    freq_index = lax.axis_index("comp") * freq_count + jnp.arange(freq_count, dtype=jnp.int32)
    scalars = (wave_speeds(freq_index, sub_counts), sub_counts, *direction_table(dir_count))
    offsets, dest = slot_table(sea_mask)
    masks = mask_planes(sea_mask, mask_low, mask_high, SUBLANES)

    done = []

    def exchange(piece):
        if done:
            piece, done[-1] = lax.optimization_barrier((piece, done[-1]))
        done.append(lax.all_to_all(piece, "comp", split_axis=0, concat_axis=0, tiled=True))
        return len(done) - 1

    def as_rows(piece):
        return piece.reshape(groups * piece.shape[1], piece.shape[2])

    chain, arrived = [], [[], []]
    for j, (start, size) in enumerate(zip(starts, sizes)):
        low, high = edges[min(j, 1)]
        low_start = 0 if j == 0 else start - sizes[0]
        moved = propagate(scalars, field, low, high, masks, start, size, low_start, chain)
        pieces = 2 if j == len(sizes) - 1 else 1
        packed = gather_points(offsets, dest, moved, start, size, groups, per_group, pieces)
        chain = [moved, packed[0]]
        packed = [exchange(piece) for piece in packed]
        for h in range(2):
            arrived[h].append((packed[h % pieces], h * half if pieces == 1 else 0))

    columns = [
        column.reshape(all_count, 1)
        for column in (growth, damping, freq_weights(*growth.shape))
    ]
    back = []
    for h in range(2):
        parts_out = [comp_count] if h == 0 else out_sizes
        increments = source_terms(
            [as_rows(done[at]) for at, _ in arrived[h]], sizes, parts_out, half,
            [lane for _, lane in arrived[h]], groups, mix_in, mix_out, columns,
        )
        for rows, size in zip(increments, parts_out):
            back.append(exchange(rows.reshape(groups, size, half)))

    for start, at in zip(out_starts, back[1:]):
        moved = scatter_points(offsets, dest, moved, done[back[0]], done[at], start)
    return moved.reshape(spectrum.shape)


def solution(mesh):
    return jax.shard_map(
        local,
        mesh=mesh,
        in_specs=(
            P("comp", None, "lat", None),
            P("lat", None),
            P("lat", None),
            P("lat"),
            P("comp"),
            P(),
            P(),
            P(),
            P(),
        ),
        out_specs=P("comp", None, "lat", None),
        check_vma=False,
    )
```

profile of v0, /device:TPU:0, one launch (start us, length us, event | category | flops | bytes accessed | tf_op | source)
XLA Modules:
  0.0 533.5 jit_solution(16056470344464112225)
XLA Ops:
  0.0 1.4 fusion.15
  2.2 1.3 collective-permute-start.3
  3.5 3.0 collective-permute-start.2
  12.5 1.0 copy-done
  13.6 21.4 %propagate.3.field_ref.refs_0_ = f32[144,96,512]{2,1,0:T(8,128)} custom-call(f32[4]{0:T(128)} %convert_divide_fusion.speed_ref, s32[4]{0:T(128)} %steps_ref.5, f32[36]{0:T(128)} %constant.24.clone.cos_ref, f32[36]{0:T(128)} %constant.11.clone.sin_ref, f32[144,96,512]{2,1,0:T(8,128)} %bitcast.38, f32[33,4,512]{2,1,0:T(4,128)} %copy-done.7, ...), custom_call_target="tpu_custom_call" | custom-call | flops 47185920 | bytes 12582912 | tf_op jit(solution)/shard_map/propagate/pallas_call | solution.py:141
  35.0 14.1 %gather_points.3.refs_1_ = bf16[8,32,4096]{2,1,0:T(8,128)(2,1)} custom-call(s32[193]{0:T(256)} %copy-done.9, f32[144,96,512]{2,1,0:T(8,128)} %propagate.3.field_ref.refs_0_, s32[192,256]{1,0:T(8,128)} %and_select_fusion.dest_ref), custom_call_target="tpu_custom_call" | custom-call | flops 805306368 | bytes 9437184 | tf_op jit(solution)/shard_map/gather_points/pallas_call | solution.py:232
  49.0 7.3 %all-to-all-start = ((bf16[8,32,4096]{2,1,0:T(8,128)(2,1)}), bf16[8,32,4096]{2,1,0:T(8,128)(2,1)}, u32[]{:S(2)}, u32[]{:S(2)}) async-start(bf16[8,32,4096]{2,1,0:T(8,128)(2,1)} %gather_points.3.refs_1_), calls=%async_computation | async-start | bytes 4194304 | tf_op jit(solution)/shard_map/all_to_all | solution.py:477
  56.3 2.5 fusion.16
  58.8 2.8 collective-permute-start
  61.6 1.3 collective-permute-start.1
  63.6 2.7 collective-permute-done.1.high_ref
  67.3 29.9 %propagate.4.field_ref.refs_0_ = f32[144,96,512]{2,1,0:T(8,128)} custom-call(f32[4]{0:T(128)} %convert_divide_fusion.speed_ref, s32[4]{0:T(128)} %steps_ref.5, f32[36]{0:T(128)} %constant.24.clone.cos_ref, f32[36]{0:T(128)} %constant.11.clone.sin_ref, f32[144,96,512]{2,1,0:T(8,128)} %bitcast.40, ...), custom_call_target="tpu_custom_call", output_to_operand_aliasing={{}: (8, {})} | custom-call | flops 70778880 | bytes 18874368 | tf_op jit(solution)/shard_map/propagate/pallas_call | solution.py:141
  97.2 15.2 %gather_points.4.refs_1_ = bf16[8,48,4096]{2,1,0:T(8,128)(2,1)} custom-call(s32[193]{0:T(256)} %copy-done.9, f32[144,96,512]{2,1,0:T(8,128)} %propagate.4.field_ref.refs_0_, s32[192,256]{1,0:T(8,128)} %and_select_fusion.dest_ref), custom_call_target="tpu_custom_call" | custom-call | flops 1207959552 | bytes 14155776 | tf_op jit(solution)/shard_map/gather_points/pallas_call | solution.py:232
  112.5 4.0 all-to-all-start.1
  116.5 30.9 %propagate.5.field_ref = f32[144,96,512]{2,1,0:T(8,128)} custom-call(f32[4]{0:T(128)} %convert_divide_fusion.speed_ref, s32[4]{0:T(128)} %steps_ref.5, f32[36]{0:T(128)} %constant.24.clone.cos_ref, f32[36]{0:T(128)} %constant.11.clone.sin_ref, f32[144,96,512]{2,1,0:T(8,128)} %bitcast.41, f32[112,4,512]{2,1,0:T(4,128)} %copy-done.2, ...), custom_call_target="tpu_custom_call", output_to_operand_aliasing={{}: (8, {})} | custom-call | flops 94371840 | bytes 25165824 | tf_op jit(solution)/shard_map/propagate/pallas_call | solution.py:141
  147.3 16.5 %gather_points.5 = (bf16[8,64,2048]{2,1,0:T(8,128)(2,1)}, bf16[8,64,2048]{2,1,0:T(8,128)(2,1)}) custom-call(s32[193]{0:T(256)} %copy-done.9, f32[144,96,512]{2,1,0:T(8,128)} %propagate.5.field_ref, s32[192,256]{1,0:T(8,128)} %and_select_fusion.dest_ref), custom_call_target="tpu_custom_call" | custom-call | flops 1610612736 | bytes 18874368 | tf_op jit(solution)/shard_map/gather_points/pallas_call | solution.py:232
  163.9 19.9 %all-to-all-done.1 = bf16[8,48,4096]{2,1,0:T(8,128)(2,1)S(1)} async-done(((bf16[8,48,4096]{2,1,0:T(8,128)(2,1)}), bf16[8,48,4096]{2,1,0:T(8,128)(2,1)S(1)}, u32[]{:S(2)}, u32[]{:S(2)}) %all-to-all-start.1) | async-done | bytes 3145760 | tf_op jit(solution)/shard_map/all_to_all | solution.py:477
  183.8 55.3 %all_to_all.35 = bf16[8,64,2048]{2,1,0:T(8,128)(2,1)} all-to-all(bf16[8,64,2048]{2,1,0:T(8,128)(2,1)} %get-tuple-element.26), channel_id=1, replica_groups=mesh['comp'=8,'lat'=4] {'comp'}, dimensions={0} | all-to-all | bytes 4194304 | tf_op jit(solution)/shard_map/all_to_all | solution.py:477
  239.1 4.5 all-to-all-start.3
  244.9 1.1 reshape_reshape.4.weight
  246.0 1.0 reshape.59.growth
  247.0 1.0 reshape.60.damping
  248.1 19.1 %source_terms.2 = bf16[1152,2048]{1,0:T(8,128)(2,1)} custom-call(bf16[1152,1152]{1,0:T(8,128)(2,1)} %mix_in.3, bf16[1152,1152]{1,0:T(8,128)(2,1)} %mix_out.3, f32[1152,1]{1,0:T(8,128)} %reshape.59.growth, f32[1152,1]{1,0:T(8,128)} %reshape.60.damping, f32[1152,1]{1,0:T(8,128)} %reshape_reshape.4.weight, bf16[256,4096]{1,0:T(8,128)(2,1)} %bitcast.15.refs_0_, ...), custom_call_target="tpu_custom_call" | custom-call | flops 10871635968 | bytes 14745600 | tf_op jit(solution)/shard_map/source_terms/pallas_call | solution.py:380
  267.2 25.4 %all-to-all-done.3 = bf16[8,64,2048]{2,1,0:T(8,128)(2,1)S(1)} async-done(((bf16[8,64,2048]{2,1,0:T(8,128)(2,1)}), bf16[8,64,2048]{2,1,0:T(8,128)(2,1)S(1)}, u32[]{:S(2)}, u32[]{:S(2)}) %all-to-all-start.3) | async-done | bytes 2097184 | tf_op jit(solution)/shard_map/all_to_all | solution.py:477
  292.7 1.3 copy-done.5
  293.9 4.6 all-to-all-start.4
  298.6 19.2 %source_terms.3 = (bf16[896,2048]{1,0:T(8,128)(2,1)}, bf16[256,2048]{1,0:T(8,128)(2,1)}) custom-call(bf16[1152,1152]{1,0:T(8,128)(2,1)} %mix_in.3, bf16[1152,1152]{1,0:T(8,128)(2,1)} %mix_out.3, f32[1152,1]{1,0:T(8,128)} %reshape.59.growth, f32[1152,1]{1,0:T(8,128)} %reshape.60.damping, f32[1152,1]{1,0:T(8,128)} %reshape_reshape.4.weight, ...), custom_call_target="tpu_custom_call" | custom-call | flops 10871635968 | bytes 14745600 | tf_op jit(solution)/shard_map/source_terms/pallas_call | solution.py:380
  317.8 85.2 %all-to-all-done.4.first_ref = bf16[8,144,2048]{2,1,0:T(8,128)(2,1)} async-done(((bf16[8,144,2048]{2,1,0:T(8,128)(2,1)}), bf16[8,144,2048]{2,1,0:T(8,128)(2,1)}, u32[]{:S(2)}, u32[]{:S(2)}) %all-to-all-start.4) | async-done | bytes 4718624 | tf_op jit(solution)/shard_map/all_to_all | solution.py:477
  403.0 86.0 %all_to_all.36.second_ref = bf16[8,112,2048]{2,1,0:T(8,128)(2,1)} all-to-all(bf16[8,112,2048]{2,1,0:T(8,128)(2,1)} %bitcast.43), channel_id=1, replica_groups=mesh['comp'=8,'lat'=4] {'comp'}, dimensions={0} | all-to-all | bytes 7340032 | tf_op jit(solution)/shard_map/all_to_all | solution.py:477
  489.0 3.6 all-to-all-start.6
  492.6 26.6 %scatter_points.2.field_ref = f32[144,96,512]{2,1,0:T(8,128)} custom-call(s32[193]{0:T(256)} %copy-done.9, f32[144,96,512]{2,1,0:T(8,128)} %propagate.5.field_ref, s32[192,256]{1,0:T(8,128)} %and_select_fusion.dest_ref, bf16[8,144,2048]{2,1,0:T(8,128)(2,1)} %all-to-all-done.4.first_ref, ...), custom_call_target="tpu_custom_call", output_to_operand_aliasing={{}: (1, {})} | custom-call | flops 2818572288 | bytes 55050240 | tf_op jit(solution)/shard_map/scatter_points/pallas_call | solution.py:311
  520.2 13.4 %scatter_points.3 = f32[144,96,512]{2,1,0:T(8,128)} custom-call(s32[193]{0:T(256)} %copy-done.9, f32[144,96,512]{2,1,0:T(8,128)} %scatter_points.2.field_ref, s32[192,256]{1,0:T(8,128)} %and_select_fusion.dest_ref, bf16[8,144,2048]{2,1,0:T(8,128)(2,1)} %all-to-all-done.4.first_ref, bf16[8,32,2048]{2,1,0:T(8,128)(2,1)} %copy-done.1), custom_call_target="tpu_custom_call", output_to_operand_aliasing={{}: (1, {})} | custom-call | flops 805306368 | bytes 15728640 | tf_op jit(solution)/shard_map/scatter_points/pallas_call | solution.py:311
  (58 shorter events, 8.8 us)
Async XLA Ops:
  0.0 6.6 %copy-start.8 = (s32[96,512]{1,0:T(8,128)S(1)}, s32[96,512]{1,0:T(8,128)}, u32[]{:S(2)}) copy-start(s32[96,512]{1,0:T(8,128)} %param.12) | copy-start | bytes 589828
  0.0 11.1 %copy-start.12 = (s32[4]{0:T(128)S(1)}, s32[4]{0:T(128)}, u32[]{:S(2)}) copy-start(s32[4]{0:T(128)} %steps_ref.5) | copy-start | bytes 52
  2.2 9.5 %collective-permute-start.3 = (f32[33,4,512]{2,1,0:T(4,128)S(1)}, f32[33,4,512]{2,1,0:T(4,128)S(1)}, u32[]{:S(2)}, u32[]{:S(2)}) collective-permute-start(f32[33,4,512]{2,1,0:T(4,128)S(1)} %pad_maximum_fusion.1), channel_id=1, source_target_pairs={{1,0},{2,1},{3,2},{5,4},{6,5},{7,6},{9,8},{10,9},{11,10},{13,12},{... | collective-permute-start | bytes 811016 | tf_op jit(solution)/shard_map/ppermute | solution.py:408
  3.5 8.2 %collective-permute-start.2 = (f32[33,4,512]{2,1,0:T(4,128)S(1)}, f32[33,4,512]{2,1,0:T(4,128)S(1)}, u32[]{:S(2)}, u32[]{:S(2)}) collective-permute-start(f32[33,4,512]{2,1,0:T(4,128)S(1)} %pad_maximum_fusion), channel_id=1, source_target_pairs={{0,1},{1,2},{2,3},{4,5},{5,6},{6,7},{8,9},{9,10},{10,11},{12,13},{... | collective-permute-start | bytes 811016 | tf_op jit(solution)/shard_map/ppermute | solution.py:408
  10.3 1.8 copy-start.9
  11.7 0.7 copy-start.6
  11.7 0.8 copy-start.7
  12.5 1.0 copy-start
  49.0 63.4 %all-to-all-start = ((bf16[8,32,4096]{2,1,0:T(8,128)(2,1)}), bf16[8,32,4096]{2,1,0:T(8,128)(2,1)}, u32[]{:S(2)}, u32[]{:S(2)}) async-start(bf16[8,32,4096]{2,1,0:T(8,128)(2,1)} %gather_points.3.refs_1_), calls=%async_computation | async-start | bytes 4194304 | tf_op jit(solution)/shard_map/all_to_all | solution.py:477
  58.8 4.8 collective-permute-start
  61.6 4.7 collective-permute-start.1
  63.6 2.7 copy-start.2
  66.4 1.0 copy-start.3
  112.5 71.3 %all-to-all-start.1 = ((bf16[8,48,4096]{2,1,0:T(8,128)(2,1)}), bf16[8,48,4096]{2,1,0:T(8,128)(2,1)S(1)}, u32[]{:S(2)}, u32[]{:S(2)}) async-start(bf16[8,48,4096]{2,1,0:T(8,128)(2,1)} %gather_points.4.refs_1_), calls=%async_computation.1 | async-start | bytes 6291456 | tf_op jit(solution)/shard_map/all_to_all | solution.py:477
  183.8 55.3 %copy-start.4 = (bf16[8,48,4096]{2,1,0:T(8,128)(2,1)}, bf16[8,48,4096]{2,1,0:T(8,128)(2,1)S(1)}, u32[]{:S(2)}) copy-start(bf16[8,48,4096]{2,1,0:T(8,128)(2,1)S(1)} %all-to-all-done.1) | copy-start | bytes 9437188
  239.1 6.9 %copy-start.10 = (f32[32,36]{1,0:T(8,128)S(1)}, f32[32,36]{1,0:T(8,128)}, u32[]{:S(2)}) copy-start(f32[32,36]{1,0:T(8,128)} %param.16) | copy-start | bytes 13828
  239.1 8.0 %copy-start.11 = (f32[32,36]{1,0:T(8,128)S(1)}, f32[32,36]{1,0:T(8,128)}, u32[]{:S(2)}) copy-start(f32[32,36]{1,0:T(8,128)} %param.17) | copy-start | bytes 13828
  239.1 53.6 %all-to-all-start.3 = ((bf16[8,64,2048]{2,1,0:T(8,128)(2,1)}), bf16[8,64,2048]{2,1,0:T(8,128)(2,1)S(1)}, u32[]{:S(2)}, u32[]{:S(2)}) async-start(bf16[8,64,2048]{2,1,0:T(8,128)(2,1)} %get-tuple-element.28), calls=%async_computation.3 | async-start | bytes 4194304 | tf_op jit(solution)/shard_map/all_to_all | solution.py:477
  292.7 1.3 copy-start.5
  293.9 109.1 %all-to-all-start.4 = ((bf16[8,144,2048]{2,1,0:T(8,128)(2,1)}), bf16[8,144,2048]{2,1,0:T(8,128)(2,1)}, u32[]{:S(2)}, u32[]{:S(2)}) async-start(bf16[8,144,2048]{2,1,0:T(8,128)(2,1)} %bitcast.42), calls=%async_computation.4 | async-start | bytes 9437184 | tf_op jit(solution)/shard_map/all_to_all | solution.py:477
  489.0 30.1 %all-to-all-start.6 = ((bf16[8,32,2048]{2,1,0:T(8,128)(2,1)}), bf16[8,32,2048]{2,1,0:T(8,128)(2,1)S(1)}, u32[]{:S(2)}, u32[]{:S(2)}) async-start(bf16[8,32,2048]{2,1,0:T(8,128)(2,1)} %bitcast.21), calls=%async_computation.6 | async-start | bytes 2097152 | tf_op jit(solution)/shard_map/all_to_all | solution.py:477
  519.2 1.0 copy-start.1
where the time goes:
time: 534 us
  Pallas kernels  206 us (39%)
  blocking collectives  141 us (26%)
  waiting for transfers between devices  134 us (25%)
  starting transfers between devices  32.4 us (6%)
  local copies, waits for them, and re-layouts  13.7 us (3%)
    all_to_all x2, blocking collectives, exchange(): lax.all_to_all(piece, 'comp', split_axis=0, concat_axis=0, tiled=True)  141 us
    all_to_all x5, waiting for transfers between devices, exchange(): lax.all_to_all(piece, 'comp', split_axis=0, concat_axis=0, tiled=True)  131 us
    pallas_call x3, Pallas kernels, propagate(): pl.pallas_call(functools.partial(propagate_kernel, start), grid_spec=pltp...  82.1 us
    pallas_call x3, Pallas kernels, gather_points(): pl.pallas_call(gather_kernel, grid_spec=pltpu.PrefetchScalarGridSpec(num_...  45.9 us
    pallas_call x2, Pallas kernels, scatter_points(): pl.pallas_call(scatter_kernel, grid_spec=pltpu.PrefetchScalarGridSpec(num...  39.9 us
    pallas_call x2, Pallas kernels, source_terms(): pl.pallas_call(functools.partial(source_kernel, counts, out_counts, group...  38.3 us
    all_to_all x5, starting transfers between devices, exchange(): lax.all_to_all(piece, 'comp', split_axis=0, concat_axis=0, tiled=True)  24 us
  transfers between devices with their start and end apart: 9, of which 5 were waited for; matrix products, arithmetic and copies ran while one was open for 2% of the time, Pallas kernels for 30%

commit v1 on v0

--- a/solution.py
+++ b/solution.py
@@ -12,6 +12,7 @@
 SUBLANES = 8
 LANES = 128
 BLOCK = 256
+STEP_ROWS = 24
 VMEM_BYTES = 56 * 1024 * 1024
 
 
@@ -78,9 +79,10 @@
         edge_col = col_id == (0 if x_up else LANES - 1)
         nothing = jnp.zeros((SUBLANES, LANES), jnp.float32)
 
-        def substep(source, target):
+        def substep(source, target=None):
             before_y = [nothing] * parts
             for s in range(strips) if y_up else range(strips - 1, -1, -1):
+                inner = 0 < s < strips - 1
                 before_x = nothing
                 for t in range(parts) if x_up else range(parts - 1, -1, -1):
                     at = (strip_rows(s), slice(t * LANES, (t + 1) * LANES))
@@ -88,28 +90,34 @@
                     turned = pltpu.roll(value, 1 if y_up else SUBLANES - 1, 0)
                     upwind_y = jnp.where(edge_row, before_y[t], turned)
                     before_y[t] = turned
+                    if target is None and not inner:
+                        continue
                     turned = pltpu.roll(value, 1 if x_up else LANES - 1, 1)
                     upwind_x = jnp.where(edge_col, before_x, turned)
                     before_x = turned
-                    target[at] = value * keep[at] + mask_ref[(0, *at)] * (
+                    moved = value * keep[at] + mask_ref[(0, *at)] * (
                         ax * upwind_x + ay * upwind_y
                     )
+                    if target is None:
+                        out_ref[(i, strip_rows(s - 1), at[1])] = moved
+                    else:
+                        target[at] = moved
 
         def pair(_, carry):
             substep(even, odd)
             substep(odd, even)
             return carry
 
-        lax.fori_loop(0, steps // 2, pair, 0)
+        lax.fori_loop(0, (steps - 1) // 2, pair, 0)
+
+        @pl.when(lax.rem(steps, 2) == 0)
+        def _():
+            substep(even, odd)
+            substep(odd)
 
         @pl.when(lax.rem(steps, 2) == 1)
         def _():
-            substep(even, odd)
-            out_ref[i] = odd[pl.ds(SUBLANES, rows), :]
-
-        @pl.when(lax.rem(steps, 2) == 0)
-        def _():
-            out_ref[i] = even[pl.ds(SUBLANES, rows), :]
+            substep(even)
 
     def component(i, carry):
         at = start + pl.program_id(0) * block + i
@@ -233,13 +241,13 @@
         gather_kernel,
         grid_spec=pltpu.PrefetchScalarGridSpec(
             num_scalar_prefetch=1,
-            grid=(rows // SUBLANES,),
+            grid=(rows // STEP_ROWS,),
             in_specs=[
                 pl.BlockSpec(
-                    (pl.Element(size), pl.Element(SUBLANES), pl.Element(cols)),
-                    lambda g, *_: (start, g * SUBLANES, 0),
+                    (pl.Element(size), pl.Element(STEP_ROWS), pl.Element(cols)),
+                    lambda g, *_: (start, g * STEP_ROWS, 0),
                 ),
-                pl.BlockSpec((SUBLANES * cols // BLOCK, BLOCK), lambda g, *_: (g, 0)),
+                pl.BlockSpec((STEP_ROWS * cols // BLOCK, BLOCK), lambda g, *_: (g, 0)),
             ],
             out_specs=[
                 pl.BlockSpec((groups, size, width), lambda g, *_: (0, 0, 0))
@@ -247,7 +255,7 @@
             ],
             scratch_shapes=[
                 pltpu.VMEM((groups + 1, size, per_group), jnp.bfloat16),
-                pltpu.VMEM((parts, size * SUBLANES, LANES), jnp.float32),
+                pltpu.VMEM((parts, size * STEP_ROWS, LANES), jnp.float32),
                 pltpu.VMEM((size, BLOCK), jnp.float32),
             ],
         ),
@@ -305,27 +313,30 @@
     rows, cols = field.shape[1:]
     parts = cols // LANES
     field_spec = pl.BlockSpec(
-        (pl.Element(size), pl.Element(SUBLANES), pl.Element(cols)),
-        lambda g, *_: (start, g * SUBLANES, 0),
+        (pl.Element(size), pl.Element(STEP_ROWS), pl.Element(cols)),
+        lambda g, *_: (start, g * STEP_ROWS, 0),
     )
     return pl.pallas_call(
         scatter_kernel,
         grid_spec=pltpu.PrefetchScalarGridSpec(
             num_scalar_prefetch=1,
-            grid=(rows // SUBLANES,),
+            grid=(rows // STEP_ROWS,),
             in_specs=[
                 field_spec,
-                pl.BlockSpec((SUBLANES * cols // BLOCK, BLOCK), lambda g, *_: (g, 0)),
+                pl.BlockSpec((STEP_ROWS * cols // BLOCK, BLOCK), lambda g, *_: (g, 0)),
                 pl.BlockSpec(
                     (pl.Element(groups), pl.Element(size), pl.Element(width)),
                     lambda g, *_: (0, start, 0),
+                    pipeline_mode=pl.Buffered(1),
                 ),
-                pl.BlockSpec((groups, size, width), lambda g, *_: (0, 0, 0)),
+                pl.BlockSpec(
+                    (groups, size, width), lambda g, *_: (0, 0, 0), pipeline_mode=pl.Buffered(1)
+                ),
             ],
             out_specs=field_spec,
             scratch_shapes=[
                 pltpu.VMEM((groups, size, 2 * width), jnp.bfloat16),
-                pltpu.VMEM((parts, size * SUBLANES, LANES), jnp.float32),
+                pltpu.VMEM((parts, size * STEP_ROWS, LANES), jnp.float32),
             ],
         ),
         out_shape=jax.ShapeDtypeStruct(field.shape, jnp.float32),
@@ -443,7 +454,7 @@
     groups = lax.axis_size("comp")
     per_group = point_index.shape[1] // groups
     half = per_group // 2
-    sizes = chunk_sizes(comp_count, (2, 3, 4))
+    sizes = chunk_sizes(comp_count, (1, 1, 1))
     starts = [sum(sizes[:j]) for j in range(len(sizes))]
     out_sizes = chunk_sizes(comp_count, (7, 2))
     out_starts = [sum(out_sizes[:j]) for j in range(len(out_sizes))]

time: 534 us -> 524 us (0.981)
  waiting for transfers between devices: 134 us -> 168 us
  Pallas kernels: 206 us -> 178 us
  blocking collectives: 141 us -> 127 us
    all_to_all x5, waiting for transfers between devices: 131 us -> 163 us  [exchange(): lax.all_to_all(piece, 'comp', split_axis=0, concat_axis=0, tiled=True)]
    all_to_all x2, blocking collectives: 141 us -> 127 us  [exchange(): lax.all_to_all(piece, 'comp', split_axis=0, concat_axis=0, tiled=True)]
    pallas_call x3, Pallas kernels: 82.1 us -> 69 us  [propagate(): pl.pallas_call(functools.partial(propagate_kernel, start), grid_spec=pltp...]
    pallas_call x3, Pallas kernels: 45.9 us -> 38.1 us  [gather_points(): pl.pallas_call(gather_kernel, grid_spec=pltpu.PrefetchScalarGridSpec(num_...]
    pallas_call x2, Pallas kernels: 39.9 us -> 32.5 us  [scatter_points(): pl.pallas_call(scatter_kernel, grid_spec=pltpu.PrefetchScalarGridSpec(num...]
  transfers between devices with their start and end apart: 9 -> 9, of which waited for: 5 -> 7; matrix products, arithmetic and copies ran while one was open for 2% -> 2% of each run, Pallas kernels for 30% -> 25%
where the time goes in v1:
time: 524 us; the launch traced here: 522 us
  Pallas kernels  178 us (34%)
  waiting for transfers between devices  168 us (32%)
  blocking collectives  127 us (24%)
  starting transfers between devices  31 us (6%)
  local copies, waits for them, and re-layouts  13.6 us (3%)
    all_to_all x5, waiting for transfers between devices, exchange(): lax.all_to_all(piece, 'comp', split_axis=0, concat_axis=0, tiled=True)  163 us
    all_to_all x2, blocking collectives, exchange(): lax.all_to_all(piece, 'comp', split_axis=0, concat_axis=0, tiled=True)  127 us
    pallas_call x3, Pallas kernels, propagate(): pl.pallas_call(functools.partial(propagate_kernel, start), grid_spec=pltp...  69 us
    pallas_call x2, Pallas kernels, source_terms(): pl.pallas_call(functools.partial(source_kernel, counts, out_counts, group...  38.4 us
    pallas_call x3, Pallas kernels, gather_points(): pl.pallas_call(gather_kernel, grid_spec=pltpu.PrefetchScalarGridSpec(num_...  38.1 us
    pallas_call x2, Pallas kernels, scatter_points(): pl.pallas_call(scatter_kernel, grid_spec=pltpu.PrefetchScalarGridSpec(num...  32.5 us
    all_to_all x5, starting transfers between devices, exchange(): lax.all_to_all(piece, 'comp', split_axis=0, concat_axis=0, tiled=True)  22.6 us
  transfers between devices with their start and end apart: 9, of which 7 were waited for; matrix products, arithmetic and copies ran while one was open for 2% of the time, Pallas kernels for 25%

profile of v1, /device:TPU:0, one launch (start us, length us, event | category | flops | bytes accessed | tf_op | source)
XLA Modules:
  0.0 522.3 jit_solution(456227590312392294)
XLA Ops:
  0.0 1.6 fusion.15
  1.7 1.3 collective-permute-start.3
  3.1 3.1 collective-permute-start.2
  13.3 26.3 %propagate.3.field_ref.refs_0_ = f32[144,96,512]{2,1,0:T(8,128)} custom-call(f32[4]{0:T(128)} %convert_divide_fusion.speed_ref, s32[4]{0:T(128)} %steps_ref.5, f32[36]{0:T(128)} %constant.24.clone.cos_ref, f32[36]{0:T(128)} %constant.11.clone.sin_ref, f32[144,96,512]{2,1,0:T(8,128)} %bitcast.38, f32[49,4,512]{2,1,0:T(4,128)} %copy-done.7, ...), custom_call_target="tpu_custom_call" | custom-call | flops 70778880 | bytes 18874368 | tf_op jit(solution)/shard_map/propagate/pallas_call | solution.py:149
  39.6 12.7 %gather_points.3.refs_1_ = bf16[8,48,4096]{2,1,0:T(8,128)(2,1)} custom-call(s32[193]{0:T(256)} %copy-done.9, f32[144,96,512]{2,1,0:T(8,128)} %propagate.3.field_ref.refs_0_, s32[192,256]{1,0:T(8,128)} %and_select_fusion.dest_ref), custom_call_target="tpu_custom_call" | custom-call | flops 1207959552 | bytes 14155776 | tf_op jit(solution)/shard_map/gather_points/pallas_call | solution.py:240
  52.3 6.7 %all-to-all-start = ((bf16[8,48,4096]{2,1,0:T(8,128)(2,1)}), bf16[8,48,4096]{2,1,0:T(8,128)(2,1)}, u32[]{:S(2)}, u32[]{:S(2)}) async-start(bf16[8,48,4096]{2,1,0:T(8,128)(2,1)} %gather_points.3.refs_1_), calls=%async_computation | async-start | bytes 6291456 | tf_op jit(solution)/shard_map/all_to_all | solution.py:488
  59.0 2.3 fusion.16
  61.3 2.8 collective-permute-start
  64.0 1.3 collective-permute-start.1
  65.9 4.1 collective-permute-done.1.high_ref
  70.9 19.0 %propagate.4.field_ref.refs_0_ = f32[144,96,512]{2,1,0:T(8,128)} custom-call(f32[4]{0:T(128)} %convert_divide_fusion.speed_ref, s32[4]{0:T(128)} %steps_ref.5, f32[36]{0:T(128)} %constant.24.clone.cos_ref, f32[36]{0:T(128)} %constant.11.clone.sin_ref, f32[144,96,512]{2,1,0:T(8,128)} %bitcast.40, ...), custom_call_target="tpu_custom_call", output_to_operand_aliasing={{}: (8, {})} | custom-call | flops 70778880 | bytes 18874368 | tf_op jit(solution)/shard_map/propagate/pallas_call | solution.py:149
  90.0 12.7 %gather_points.4.refs_1_ = bf16[8,48,4096]{2,1,0:T(8,128)(2,1)} custom-call(s32[193]{0:T(256)} %copy-done.9, f32[144,96,512]{2,1,0:T(8,128)} %propagate.4.field_ref.refs_0_, s32[192,256]{1,0:T(8,128)} %and_select_fusion.dest_ref), custom_call_target="tpu_custom_call" | custom-call | flops 1207959552 | bytes 14155776 | tf_op jit(solution)/shard_map/gather_points/pallas_call | solution.py:240
  102.6 28.6 %all-to-all-done = bf16[8,48,4096]{2,1,0:T(8,128)(2,1)} async-done(((bf16[8,48,4096]{2,1,0:T(8,128)(2,1)}), bf16[8,48,4096]{2,1,0:T(8,128)(2,1)}, u32[]{:S(2)}, u32[]{:S(2)}) %all-to-all-start) | async-done | bytes 3145760 | tf_op jit(solution)/shard_map/all_to_all | solution.py:488
  131.3 3.8 all-to-all-start.1
  135.1 23.6 %propagate.5.field_ref = f32[144,96,512]{2,1,0:T(8,128)} custom-call(f32[4]{0:T(128)} %convert_divide_fusion.speed_ref, s32[4]{0:T(128)} %steps_ref.5, f32[36]{0:T(128)} %constant.24.clone.cos_ref, f32[36]{0:T(128)} %constant.11.clone.sin_ref, f32[144,96,512]{2,1,0:T(8,128)} %bitcast.41, f32[96,4,512]{2,1,0:T(4,128)} %copy-done.2, ...), custom_call_target="tpu_custom_call", output_to_operand_aliasing={{}: (8, {})} | custom-call | flops 70778880 | bytes 18874368 | tf_op jit(solution)/shard_map/propagate/pallas_call | solution.py:149
  158.7 12.7 %gather_points.5 = (bf16[8,48,2048]{2,1,0:T(8,128)(2,1)}, bf16[8,48,2048]{2,1,0:T(8,128)(2,1)}) custom-call(s32[193]{0:T(256)} %copy-done.9, f32[144,96,512]{2,1,0:T(8,128)} %propagate.5.field_ref, s32[192,256]{1,0:T(8,128)} %and_select_fusion.dest_ref), custom_call_target="tpu_custom_call" | custom-call | flops 1207959552 | bytes 14155776 | tf_op jit(solution)/shard_map/gather_points/pallas_call | solution.py:240
  171.4 34.5 %all-to-all-done.1 = bf16[8,48,4096]{2,1,0:T(8,128)(2,1)S(1)} async-done(((bf16[8,48,4096]{2,1,0:T(8,128)(2,1)}), bf16[8,48,4096]{2,1,0:T(8,128)(2,1)S(1)}, u32[]{:S(2)}, u32[]{:S(2)}) %all-to-all-start.1) | async-done | bytes 3145760 | tf_op jit(solution)/shard_map/all_to_all | solution.py:488
  206.0 40.9 %all_to_all.35 = bf16[8,48,2048]{2,1,0:T(8,128)(2,1)} all-to-all(bf16[8,48,2048]{2,1,0:T(8,128)(2,1)} %get-tuple-element.26), channel_id=1, replica_groups=mesh['comp'=8,'lat'=4] {'comp'}, dimensions={0} | all-to-all | bytes 3145728 | tf_op jit(solution)/shard_map/all_to_all | solution.py:488
  246.9 3.7 all-to-all-start.3
  251.9 1.0 reshape_reshape.4.weight
  252.9 1.0 reshape.59.growth
  255.0 19.2 %source_terms.2 = bf16[1152,2048]{1,0:T(8,128)(2,1)} custom-call(bf16[1152,1152]{1,0:T(8,128)(2,1)} %mix_in.3, bf16[1152,1152]{1,0:T(8,128)(2,1)} %mix_out.3, f32[1152,1]{1,0:T(8,128)} %reshape.59.growth, f32[1152,1]{1,0:T(8,128)} %reshape.60.damping, f32[1152,1]{1,0:T(8,128)} %reshape_reshape.4.weight, bf16[384,4096]{1,0:T(8,128)(2,1)} %bitcast.15.refs_0_, ...), custom_call_target="tpu_custom_call" | custom-call | flops 10871635968 | bytes 14745600 | tf_op jit(solution)/shard_map/source_terms/pallas_call | solution.py:391
  274.2 12.9 %all-to-all-done.3 = bf16[8,48,2048]{2,1,0:T(8,128)(2,1)S(1)} async-done(((bf16[8,48,2048]{2,1,0:T(8,128)(2,1)}), bf16[8,48,2048]{2,1,0:T(8,128)(2,1)S(1)}, u32[]{:S(2)}, u32[]{:S(2)}) %all-to-all-start.3) | async-done | bytes 1572896 | tf_op jit(solution)/shard_map/all_to_all | solution.py:488
  287.1 1.2 copy-done.5
  288.3 4.6 all-to-all-start.4
  292.9 19.1 %source_terms.3 = (bf16[896,2048]{1,0:T(8,128)(2,1)}, bf16[256,2048]{1,0:T(8,128)(2,1)}) custom-call(bf16[1152,1152]{1,0:T(8,128)(2,1)} %mix_in.3, bf16[1152,1152]{1,0:T(8,128)(2,1)} %mix_out.3, f32[1152,1]{1,0:T(8,128)} %reshape.59.growth, f32[1152,1]{1,0:T(8,128)} %reshape.60.damping, f32[1152,1]{1,0:T(8,128)} %reshape_reshape.4.weight, ...), custom_call_target="tpu_custom_call" | custom-call | flops 10871635968 | bytes 14745600 | tf_op jit(solution)/shard_map/source_terms/pallas_call | solution.py:391
  312.0 84.6 %all-to-all-done.4.first_ref = bf16[8,144,2048]{2,1,0:T(8,128)(2,1)} async-done(((bf16[8,144,2048]{2,1,0:T(8,128)(2,1)}), bf16[8,144,2048]{2,1,0:T(8,128)(2,1)}, u32[]{:S(2)}, u32[]{:S(2)}) %all-to-all-start.4) | async-done | bytes 4718624 | tf_op jit(solution)/shard_map/all_to_all | solution.py:488
  396.6 86.0 %all_to_all.36.second_ref = bf16[8,112,2048]{2,1,0:T(8,128)(2,1)} all-to-all(bf16[8,112,2048]{2,1,0:T(8,128)(2,1)} %bitcast.43), channel_id=1, replica_groups=mesh['comp'=8,'lat'=4] {'comp'}, dimensions={0} | all-to-all | bytes 7340032 | tf_op jit(solution)/shard_map/all_to_all | solution.py:488
  482.6 3.8 all-to-all-start.6
  486.4 22.8 %scatter_points.2.field_ref = f32[144,96,512]{2,1,0:T(8,128)} custom-call(s32[193]{0:T(256)} %copy-done.9, f32[144,96,512]{2,1,0:T(8,128)} %propagate.5.field_ref, s32[192,256]{1,0:T(8,128)} %and_select_fusion.dest_ref, bf16[8,144,2048]{2,1,0:T(8,128)(2,1)} %all-to-all-done.4.first_ref, ...), custom_call_target="tpu_custom_call", output_to_operand_aliasing={{}: (1, {})} | custom-call | flops 2818572288 | bytes 55050240 | tf_op jit(solution)/shard_map/scatter_points/pallas_call | solution.py:319
  509.2 2.4 all-to-all-done.6.second_ref
  512.6 9.7 %scatter_points.3 = f32[144,96,512]{2,1,0:T(8,128)} custom-call(s32[193]{0:T(256)} %copy-done.9, f32[144,96,512]{2,1,0:T(8,128)} %scatter_points.2.field_ref, s32[192,256]{1,0:T(8,128)} %and_select_fusion.dest_ref, bf16[8,144,2048]{2,1,0:T(8,128)(2,1)} %all-to-all-done.4.first_ref, bf16[8,32,2048]{2,1,0:T(8,128)(2,1)} %copy-done.1), custom_call_target="tpu_custom_call", output_to_operand_aliasing={{}: (1, {})} | custom-call | flops 805306368 | bytes 15728640 | tf_op jit(solution)/shard_map/scatter_points/pallas_call | solution.py:319
  (58 shorter events, 10.1 us)
Async XLA Ops:
  0.0 1.6 copy-start.8
  1.7 9.0 %copy-start.12 = (s32[4]{0:T(128)S(1)}, s32[4]{0:T(128)}, u32[]{:S(2)}) copy-start(s32[4]{0:T(128)} %steps_ref.5) | copy-start | bytes 52
  1.7 9.6 %collective-permute-start.3 = (f32[49,4,512]{2,1,0:T(4,128)S(1)}, f32[49,4,512]{2,1,0:T(4,128)S(1)}, u32[]{:S(2)}, u32[]{:S(2)}) collective-permute-start(f32[49,4,512]{2,1,0:T(4,128)S(1)} %pad_maximum_fusion.1), channel_id=1, source_target_pairs={{1,0},{2,1},{3,2},{5,4},{6,5},{7,6},{9,8},{10,9},{11,10},{13,12},{... | collective-permute-start | bytes 1204232 | tf_op jit(solution)/shard_map/ppermute | solution.py:419
  3.1 8.2 %collective-permute-start.2 = (f32[49,4,512]{2,1,0:T(4,128)S(1)}, f32[49,4,512]{2,1,0:T(4,128)S(1)}, u32[]{:S(2)}, u32[]{:S(2)}) collective-permute-start(f32[49,4,512]{2,1,0:T(4,128)S(1)} %pad_maximum_fusion), channel_id=1, source_target_pairs={{0,1},{1,2},{2,3},{4,5},{5,6},{6,7},{8,9},{9,10},{10,11},{12,13},{... | collective-permute-start | bytes 1204232 | tf_op jit(solution)/shard_map/ppermute | solution.py:419
  9.9 1.7 copy-start.9
  11.3 0.8 copy-start.6
  11.3 0.9 copy-start.7
  12.3 1.0 copy-start
  52.3 78.9 %all-to-all-start = ((bf16[8,48,4096]{2,1,0:T(8,128)(2,1)}), bf16[8,48,4096]{2,1,0:T(8,128)(2,1)}, u32[]{:S(2)}, u32[]{:S(2)}) async-start(bf16[8,48,4096]{2,1,0:T(8,128)(2,1)} %gather_points.3.refs_1_), calls=%async_computation | async-start | bytes 6291456 | tf_op jit(solution)/shard_map/all_to_all | solution.py:488
  61.3 4.6 collective-permute-start
  64.0 5.9 %collective-permute-start.1 = (f32[96,4,512]{2,1,0:T(4,128)S(1)}, f32[96,4,512]{2,1,0:T(4,128)S(1)}, u32[]{:S(2)}, u32[]{:S(2)}) collective-permute-start(f32[96,4,512]{2,1,0:T(4,128)S(1)} %get-tuple-element.39), channel_id=1, source_target_pairs={{1,0},{2,1},{3,2},{5,4},{6,5},{7,6},{9,8},{10,9},{11,10},{13,12},{... | collective-permute-start | bytes 2359304 | tf_op jit(solution)/shard_map/ppermute | solution.py:419
  65.9 4.1 copy-start.2
  70.0 1.0 copy-start.3
  131.3 74.7 %all-to-all-start.1 = ((bf16[8,48,4096]{2,1,0:T(8,128)(2,1)}), bf16[8,48,4096]{2,1,0:T(8,128)(2,1)S(1)}, u32[]{:S(2)}, u32[]{:S(2)}) async-start(bf16[8,48,4096]{2,1,0:T(8,128)(2,1)} %gather_points.4.refs_1_), calls=%async_computation.1 | async-start | bytes 6291456 | tf_op jit(solution)/shard_map/all_to_all | solution.py:488
  206.0 41.0 %copy-start.4 = (bf16[8,48,4096]{2,1,0:T(8,128)(2,1)}, bf16[8,48,4096]{2,1,0:T(8,128)(2,1)S(1)}, u32[]{:S(2)}) copy-start(bf16[8,48,4096]{2,1,0:T(8,128)(2,1)S(1)} %all-to-all-done.1) | copy-start | bytes 9437188
  246.9 6.0 %copy-start.10 = (f32[32,36]{1,0:T(8,128)S(1)}, f32[32,36]{1,0:T(8,128)}, u32[]{:S(2)}) copy-start(f32[32,36]{1,0:T(8,128)} %param.16) | copy-start | bytes 13828
  246.9 7.0 %copy-start.11 = (f32[32,36]{1,0:T(8,128)S(1)}, f32[32,36]{1,0:T(8,128)}, u32[]{:S(2)}) copy-start(f32[32,36]{1,0:T(8,128)} %param.17) | copy-start | bytes 13828
  246.9 40.2 %all-to-all-start.3 = ((bf16[8,48,2048]{2,1,0:T(8,128)(2,1)}), bf16[8,48,2048]{2,1,0:T(8,128)(2,1)S(1)}, u32[]{:S(2)}, u32[]{:S(2)}) async-start(bf16[8,48,2048]{2,1,0:T(8,128)(2,1)} %get-tuple-element.28), calls=%async_computation.3 | async-start | bytes 3145728 | tf_op jit(solution)/shard_map/all_to_all | solution.py:488
  287.1 1.2 copy-start.5
  288.3 108.4 %all-to-all-start.4 = ((bf16[8,144,2048]{2,1,0:T(8,128)(2,1)}), bf16[8,144,2048]{2,1,0:T(8,128)(2,1)}, u32[]{:S(2)}, u32[]{:S(2)}) async-start(bf16[8,144,2048]{2,1,0:T(8,128)(2,1)} %bitcast.42), calls=%async_computation.4 | async-start | bytes 9437184 | tf_op jit(solution)/shard_map/all_to_all | solution.py:488
  482.6 28.9 %all-to-all-start.6 = ((bf16[8,32,2048]{2,1,0:T(8,128)(2,1)}), bf16[8,32,2048]{2,1,0:T(8,128)(2,1)S(1)}, u32[]{:S(2)}, u32[]{:S(2)}) async-start(bf16[8,32,2048]{2,1,0:T(8,128)(2,1)} %bitcast.21), calls=%async_computation.6 | async-start | bytes 2097152 | tf_op jit(solution)/shard_map/all_to_all | solution.py:488
  511.6 1.0 copy-start.1

commit v2 on v1

--- a/solution.py
+++ b/solution.py
@@ -13,6 +13,7 @@
 LANES = 128
 BLOCK = 256
 STEP_ROWS = 24
+SPREAD = 16
 VMEM_BYTES = 56 * 1024 * 1024
 
 
@@ -137,12 +138,12 @@
     lax.fori_loop(0, block, component, 0)
 
 
-def propagate(scalars, spectrum, low, high, masks, start, size, low_start, chain):
+def propagate(scalars, spectrum, low, high, masks, start, size, chain):
     comp_count, rows, cols = spectrum.shape
     halo = low.shape[1]
     block = next(
         n for n in range(min(16, size), 0, -1)
-        if size % n == 0 and start % n == 0 and low_start % n == 0
+        if size % n == 0 and start % n == 0
     )
     ext = masks.shape[1]
     cells = size * rows * cols
@@ -153,8 +154,8 @@
             grid=(size // block,),
             in_specs=[
                 pl.BlockSpec((block, rows, cols), lambda g, *_: (start // block + g, 0, 0)),
-                pl.BlockSpec((block, halo, cols), lambda g, *_: (low_start // block + g, 0, 0)),
-                pl.BlockSpec((block, halo, cols), lambda g, *_: (low_start // block + g, 0, 0)),
+                pl.BlockSpec((block, halo, cols), lambda g, *_: (g, 0, 0)),
+                pl.BlockSpec((block, halo, cols), lambda g, *_: (g, 0, 0)),
                 pl.BlockSpec(masks.shape, lambda g, *_: (0, 0, 0)),
             ]
             + [pl.BlockSpec(memory_space=pl.ANY) for _ in chain],
@@ -171,11 +172,12 @@
     )(*scalars, spectrum, low, high, masks, *chain)
 
 
-def selection(dest_row):
+def selection(dest):
+    spread = dest.shape[0]
     slot = lax.broadcasted_iota(jnp.int32, (BLOCK, BLOCK), 0)
-    slot = slot.astype(jnp.float32).astype(jnp.bfloat16)
+    slot = slot.astype(jnp.float32).astype(jnp.bfloat16).reshape(BLOCK // spread, spread, BLOCK)
     one, zero = jnp.ones((), jnp.bfloat16), jnp.zeros((), jnp.bfloat16)
-    return jnp.where(slot == dest_row.astype(jnp.float32).astype(jnp.bfloat16), one, zero)
+    return jnp.where(slot == dest[None], one, zero).reshape(BLOCK, BLOCK)
 
 
 def tile_of(offset):
@@ -215,7 +217,7 @@
             [rows_of[t + i, pl.ds(r, size, stride=rows), :] for i in range(BLOCK // LANES)], axis=1
         ).astype(jnp.bfloat16)
         placed = lax.dot_general(
-            values, selection(dest_ref[pl.ds(b, 1), :]), (((1,), (1,)), ((), ())),
+            values, selection(dest_ref[b]), (((1,), (1,)), ((), ())),
             preferred_element_type=jnp.float32,
         )
         offset, following = offset_ref[first_block + b], offset_ref[first_block + b + 1]
@@ -247,7 +249,7 @@
                     (pl.Element(size), pl.Element(STEP_ROWS), pl.Element(cols)),
                     lambda g, *_: (start, g * STEP_ROWS, 0),
                 ),
-                pl.BlockSpec((STEP_ROWS * cols // BLOCK, BLOCK), lambda g, *_: (g, 0)),
+                pl.BlockSpec((STEP_ROWS * cols // BLOCK, *dest.shape[1:]), lambda g, *_: (g, 0, 0)),
             ],
             out_specs=[
                 pl.BlockSpec((groups, size, width), lambda g, *_: (0, 0, 0))
@@ -299,7 +301,7 @@
             packed[tile_place(following, per_group)],
         )
         found = jnp.dot(
-            values, selection(dest_ref[pl.ds(b, 1), :]), preferred_element_type=jnp.float32
+            values, selection(dest_ref[b]), preferred_element_type=jnp.float32
         )
         for i in range(BLOCK // LANES):
             rows_of[t + i, pl.ds(r, size, stride=rows), :] = found[:, i * LANES:(i + 1) * LANES]
@@ -323,7 +325,7 @@
             grid=(rows // STEP_ROWS,),
             in_specs=[
                 field_spec,
-                pl.BlockSpec((STEP_ROWS * cols // BLOCK, BLOCK), lambda g, *_: (g, 0)),
+                pl.BlockSpec((STEP_ROWS * cols // BLOCK, *dest.shape[1:]), lambda g, *_: (g, 0, 0)),
                 pl.BlockSpec(
                     (pl.Element(groups), pl.Element(size), pl.Element(width)),
                     lambda g, *_: (0, start, 0),
@@ -442,7 +444,8 @@
     offset = jnp.dot(before, count, precision=lax.Precision.HIGHEST)
     offset = jnp.append(offset, offset[-1] + count[-1]).astype(jnp.int32)
     place = lane_of(rank.astype(jnp.int32) - 1 + offset[:-1, None])
-    return offset, jnp.where(cells > 0.0, place, -1)
+    place = jnp.where(cells > 0.0, place, -1).astype(jnp.float32).astype(jnp.bfloat16)
+    return offset, jnp.broadcast_to(place[:, None, :], (blocks, SPREAD, BLOCK))
 
 
 def local(
@@ -454,7 +457,7 @@
     groups = lax.axis_size("comp")
     per_group = point_index.shape[1] // groups
     half = per_group // 2
-    sizes = chunk_sizes(comp_count, (1, 1, 1))
+    sizes = chunk_sizes(comp_count, (2, 3, 4))
     starts = [sum(sizes[:j]) for j in range(len(sizes))]
     out_sizes = chunk_sizes(comp_count, (7, 2))
     out_starts = [sum(out_sizes[:j]) for j in range(len(out_sizes))]
@@ -466,14 +469,15 @@
         mask_rows = sea_mask[at].astype(jnp.float32)
         return jnp.concatenate([field[:sizes[0], at], mask_rows[None]], axis=0)
 
-    def later_edge(last):
-        at = slice(row_count - NSUB, row_count) if last else slice(0, NSUB)
-        return field[sizes[0]:, at]
-
-    edges = [edge_rows(first_edge, "lat")]
-    if len(sizes) > 1:
-        edges.append(edge_rows(later_edge, "lat"))
-    mask_low, mask_high = edges[0][0][sizes[0]], edges[0][1][sizes[0]]
+    def later_edges(start, size, after):
+        def later_edge(last):
+            at = slice(row_count - NSUB, row_count) if last else slice(0, NSUB)
+            return lax.optimization_barrier((field[start:start + size, at], after))[0]
+
+        return edge_rows(later_edge, "lat")
+
+    first_edges = edge_rows(first_edge, "lat")
+    mask_low, mask_high = first_edges[0][sizes[0]], first_edges[1][sizes[0]]
 
     freq_index = lax.axis_index("comp") * freq_count + jnp.arange(freq_count, dtype=jnp.int32)
     scalars = (wave_speeds(freq_index, sub_counts), sub_counts, *direction_table(dir_count))
@@ -493,9 +497,8 @@
 
     chain, arrived = [], [[], []]
     for j, (start, size) in enumerate(zip(starts, sizes)):
-        low, high = edges[min(j, 1)]
-        low_start = 0 if j == 0 else start - sizes[0]
-        moved = propagate(scalars, field, low, high, masks, start, size, low_start, chain)
+        low, high = later_edges(start, size, chain[1]) if j > 0 else first_edges
+        moved = propagate(scalars, field, low, high, masks, start, size, chain)
         pieces = 2 if j == len(sizes) - 1 else 1
         packed = gather_points(offsets, dest, moved, start, size, groups, per_group, pieces)
         chain = [moved, packed[0]]

time: 524 us -> 522 us (level)
  waiting for transfers between devices: 168 us -> 138 us
  blocking collectives: 127 us -> 142 us
  starting transfers between devices: 31 us -> 38.5 us
    all_to_all x5, waiting for transfers between devices: 163 us -> 135 us  [exchange(): lax.all_to_all(piece, 'comp', split_axis=0, concat_axis=0, tiled=True)]
    all_to_all x2, blocking collectives: 127 us -> 142 us  [exchange(): lax.all_to_all(piece, 'comp', split_axis=0, concat_axis=0, tiled=True)]
    ppermute x2 -> x3, starting transfers between devices: 5.82 us -> 13.5 us  [edge_rows(): lax.ppermute(make(True), axis, forward)]
  transfers between devices with their start and end apart: 9 -> 11, of which waited for: 7 -> 7; matrix products, arithmetic and copies ran while one was open for 2% -> 2% of each run, Pallas kernels for 25% -> 26%
where the time goes in v2:
time: 522 us; the launch traced here: 520 us
  Pallas kernels  178 us (34%)
  blocking collectives  142 us (27%)
  waiting for transfers between devices  138 us (26%)
  starting transfers between devices  38.5 us (7%)
  local copies, waits for them, and re-layouts  17.7 us (3%)
    all_to_all x2, blocking collectives, exchange(): lax.all_to_all(piece, 'comp', split_axis=0, concat_axis=0, tiled=True)  142 us
    all_to_all x5, waiting for transfers between devices, exchange(): lax.all_to_all(piece, 'comp', split_axis=0, concat_axis=0, tiled=True)  135 us
    pallas_call x3, Pallas kernels, propagate(): pl.pallas_call(functools.partial(propagate_kernel, start), grid_spec=pltp...  69 us
    pallas_call x2, Pallas kernels, source_terms(): pl.pallas_call(functools.partial(source_kernel, counts, out_counts, group...  38.3 us
    pallas_call x3, Pallas kernels, gather_points(): pl.pallas_call(gather_kernel, grid_spec=pltpu.PrefetchScalarGridSpec(num_...  38.2 us
    pallas_call x2, Pallas kernels, scatter_points(): pl.pallas_call(scatter_kernel, grid_spec=pltpu.PrefetchScalarGridSpec(num...  32.9 us
    all_to_all x5, starting transfers between devices, exchange(): lax.all_to_all(piece, 'comp', split_axis=0, concat_axis=0, tiled=True)  21.1 us
    ppermute x3, starting transfers between devices, edge_rows(): lax.ppermute(make(True), axis, forward)  13.5 us
  transfers between devices with their start and end apart: 11, of which 7 were waited for; matrix products, arithmetic and copies ran while one was open for 2% of the time, Pallas kernels for 26%

profile of v2, /device:TPU:0, one launch (start us, length us, event | category | flops | bytes accessed | tf_op | source)
XLA Modules:
  0.0 520.0 jit_solution(3140655201267941603)
XLA Ops:
  0.0 1.4 fusion.17
  3.5 3.0 collective-permute-start
  12.8 20.7 %propagate.3.field_ref.refs_0_ = f32[144,96,512]{2,1,0:T(8,128)} custom-call(f32[4]{0:T(128)} %convert_divide_fusion.speed_ref, s32[4]{0:T(128)} %steps_ref.5, f32[36]{0:T(128)} %constant.24.clone.cos_ref, f32[36]{0:T(128)} %constant.11.clone.sin_ref, f32[144,96,512]{2,1,0:T(8,128)} %bitcast.38, f32[33,4,512]{2,1,0:T(4,128)} %copy-done.10, ...), custom_call_target="tpu_custom_call" | custom-call | flops 47185920 | bytes 12582912 | tf_op jit(solution)/shard_map/propagate/pallas_call | solution.py:150
  33.5 1.3 broadcast_in_dim.44.dest_ref
  34.8 11.8 %gather_points.3.refs_1_ = bf16[8,32,4096]{2,1,0:T(8,128)(2,1)} custom-call(s32[193]{0:T(256)} %copy-done.12, f32[144,96,512]{2,1,0:T(8,128)} %propagate.3.field_ref.refs_0_, bf16[192,16,256]{2,1,0:T(8,128)(2,1)} %broadcast_in_dim.44.dest_ref), custom_call_target="tpu_custom_call" | custom-call | flops 805306368 | bytes 9437184 | tf_op jit(solution)/shard_map/gather_points/pallas_call | solution.py:242
  46.6 5.3 %all-to-all-start = ((bf16[8,32,4096]{2,1,0:T(8,128)(2,1)}), bf16[8,32,4096]{2,1,0:T(8,128)(2,1)S(1)}, u32[]{:S(2)}, u32[]{:S(2)}) async-start(bf16[8,32,4096]{2,1,0:T(8,128)(2,1)} %gather_points.3.refs_1_), calls=%async_computation | async-start | bytes 4194304 | tf_op jit(solution)/shard_map/all_to_all | solution.py:492
  51.9 1.6 fusion.16
  53.5 1.3 collective-permute-start.3
  54.8 3.4 collective-permute-start.2
  60.2 19.9 %propagate.4.field_ref.refs_0_ = f32[144,96,512]{2,1,0:T(8,128)} custom-call(f32[4]{0:T(128)} %convert_divide_fusion.speed_ref, s32[4]{0:T(128)} %steps_ref.5, f32[36]{0:T(128)} %constant.24.clone.cos_ref, f32[36]{0:T(128)} %constant.11.clone.sin_ref, f32[144,96,512]{2,1,0:T(8,128)} %bitcast.40, ...), custom_call_target="tpu_custom_call", output_to_operand_aliasing={{}: (8, {})} | custom-call | flops 70778880 | bytes 18874368 | tf_op jit(solution)/shard_map/propagate/pallas_call | solution.py:150
  80.1 12.7 %gather_points.4.refs_1_ = bf16[8,48,4096]{2,1,0:T(8,128)(2,1)} custom-call(s32[193]{0:T(256)} %copy-done.12, f32[144,96,512]{2,1,0:T(8,128)} %propagate.4.field_ref.refs_0_, bf16[192,16,256]{2,1,0:T(8,128)(2,1)} %broadcast_in_dim.44.dest_ref), custom_call_target="tpu_custom_call" | custom-call | flops 1207959552 | bytes 14155776 | tf_op jit(solution)/shard_map/gather_points/pallas_call | solution.py:242
  92.8 8.8 %all-to-all-done = bf16[8,32,4096]{2,1,0:T(8,128)(2,1)S(1)} async-done(((bf16[8,32,4096]{2,1,0:T(8,128)(2,1)}), bf16[8,32,4096]{2,1,0:T(8,128)(2,1)S(1)}, u32[]{:S(2)}, u32[]{:S(2)}) %all-to-all-start) | async-done | bytes 2097184 | tf_op jit(solution)/shard_map/all_to_all | solution.py:492
  101.6 1.3 copy-done.3
  102.9 3.6 all-to-all-start.1
  106.6 1.8 fusion.15
  109.7 7.1 %collective-permute-start.4 = (f32[64,4,512]{2,1,0:T(4,128)S(1)}, f32[64,4,512]{2,1,0:T(4,128)S(1)}, u32[]{:S(2)}, u32[]{:S(2)}) collective-permute-start(f32[64,4,512]{2,1,0:T(4,128)S(1)} %get-tuple-element.27), channel_id=1, source_target_pairs={{0,1},{1,2},{2,3},{4,5},{5,6},{6,7},{8,9},{9,10},{10,11},{12,13},{... | collective-permute-start | bytes 1572872 | tf_op jit(solution)/shard_map/ppermute | solution.py:421
  118.9 28.4 %propagate.5.field_ref = f32[144,96,512]{2,1,0:T(8,128)} custom-call(f32[4]{0:T(128)} %convert_divide_fusion.speed_ref, s32[4]{0:T(128)} %steps_ref.5, f32[36]{0:T(128)} %constant.24.clone.cos_ref, f32[36]{0:T(128)} %constant.11.clone.sin_ref, f32[144,96,512]{2,1,0:T(8,128)} %bitcast.42, f32[64,4,512]{2,1,0:T(4,128)} %copy-done.6, ...), custom_call_target="tpu_custom_call", output_to_operand_aliasing={{}: (8, {})} | custom-call | flops 94371840 | bytes 25165824 | tf_op jit(solution)/shard_map/propagate/pallas_call | solution.py:150
  147.3 13.7 %gather_points.5 = (bf16[8,64,2048]{2,1,0:T(8,128)(2,1)}, bf16[8,64,2048]{2,1,0:T(8,128)(2,1)}) custom-call(s32[193]{0:T(256)} %copy-done.12, f32[144,96,512]{2,1,0:T(8,128)} %propagate.5.field_ref, bf16[192,16,256]{2,1,0:T(8,128)(2,1)} %broadcast_in_dim.44.dest_ref), custom_call_target="tpu_custom_call" | custom-call | flops 1610612736 | bytes 18874368 | tf_op jit(solution)/shard_map/gather_points/pallas_call | solution.py:242
  161.0 14.6 %all-to-all-done.1 = bf16[8,48,4096]{2,1,0:T(8,128)(2,1)S(1)} async-done(((bf16[8,48,4096]{2,1,0:T(8,128)(2,1)}), bf16[8,48,4096]{2,1,0:T(8,128)(2,1)S(1)}, u32[]{:S(2)}, u32[]{:S(2)}) %all-to-all-start.1) | async-done | bytes 3145760 | tf_op jit(solution)/shard_map/all_to_all | solution.py:492
  175.6 56.4 %all_to_all.35 = bf16[8,64,2048]{2,1,0:T(8,128)(2,1)} all-to-all(bf16[8,64,2048]{2,1,0:T(8,128)(2,1)} %get-tuple-element.34), channel_id=1, replica_groups=mesh['comp'=8,'lat'=4] {'comp'}, dimensions={0} | all-to-all | bytes 4194304 | tf_op jit(solution)/shard_map/all_to_all | solution.py:492
  231.9 3.8 all-to-all-start.3
  240.2 19.1 %source_terms.2 = bf16[1152,2048]{1,0:T(8,128)(2,1)} custom-call(bf16[1152,1152]{1,0:T(8,128)(2,1)} %mix_in.3, bf16[1152,1152]{1,0:T(8,128)(2,1)} %mix_out.3, f32[1152,1]{1,0:T(8,128)} %reshape.60.growth, f32[1152,1]{1,0:T(8,128)} %reshape.61.damping, f32[1152,1]{1,0:T(8,128)} %reshape_reshape.4.weight, bf16[256,4096]{1,0:T(8,128)(2,1)} %bitcast.47, ...), custom_call_target="tpu_custom_call" | custom-call | flops 10871635968 | bytes 14745600 | tf_op jit(solution)/shard_map/source_terms/pallas_call | solution.py:393
  259.3 25.0 %all-to-all-done.3 = bf16[8,64,2048]{2,1,0:T(8,128)(2,1)S(1)} async-done(((bf16[8,64,2048]{2,1,0:T(8,128)(2,1)}), bf16[8,64,2048]{2,1,0:T(8,128)(2,1)S(1)}, u32[]{:S(2)}, u32[]{:S(2)}) %all-to-all-start.3) | async-done | bytes 2097184 | tf_op jit(solution)/shard_map/all_to_all | solution.py:492
  284.3 1.3 copy-done.4
  285.6 4.6 all-to-all-start.4
  290.2 19.2 %source_terms.3 = (bf16[896,2048]{1,0:T(8,128)(2,1)}, bf16[256,2048]{1,0:T(8,128)(2,1)}) custom-call(bf16[1152,1152]{1,0:T(8,128)(2,1)} %mix_in.3, bf16[1152,1152]{1,0:T(8,128)(2,1)} %mix_out.3, f32[1152,1]{1,0:T(8,128)} %reshape.60.growth, f32[1152,1]{1,0:T(8,128)} %reshape.61.damping, f32[1152,1]{1,0:T(8,128)} %reshape_reshape.4.weight, ...), custom_call_target="tpu_custom_call" | custom-call | flops 10871635968 | bytes 14745600 | tf_op jit(solution)/shard_map/source_terms/pallas_call | solution.py:393
  309.4 84.8 %all-to-all-done.4.first_ref = bf16[8,144,2048]{2,1,0:T(8,128)(2,1)} async-done(((bf16[8,144,2048]{2,1,0:T(8,128)(2,1)}), bf16[8,144,2048]{2,1,0:T(8,128)(2,1)}, u32[]{:S(2)}, u32[]{:S(2)}) %all-to-all-start.4) | async-done | bytes 4718624 | tf_op jit(solution)/shard_map/all_to_all | solution.py:492
  394.2 86.0 %all_to_all.36.second_ref = bf16[8,112,2048]{2,1,0:T(8,128)(2,1)} all-to-all(bf16[8,112,2048]{2,1,0:T(8,128)(2,1)} %bitcast.44), channel_id=1, replica_groups=mesh['comp'=8,'lat'=4] {'comp'}, dimensions={0} | all-to-all | bytes 7340032 | tf_op jit(solution)/shard_map/all_to_all | solution.py:492
  480.2 3.8 all-to-all-start.6
  484.0 23.0 %scatter_points.2.field_ref = f32[144,96,512]{2,1,0:T(8,128)} custom-call(s32[193]{0:T(256)} %copy-done.12, f32[144,96,512]{2,1,0:T(8,128)} %propagate.5.field_ref, bf16[192,16,256]{2,1,0:T(8,128)(2,1)} %broadcast_in_dim.44.dest_ref, bf16[8,144,2048]{2,1,0:T(8,128)(2,1)} %all-to-all-done.4.first_ref, ...), custom_call_target="tpu_custom_call", output_to_operand_aliasing={{}: (1, {})} | custom-call | flops 2818572288 | bytes 55050240 | tf_op jit(solution)/shard_map/scatter_points/pallas_call | solution.py:321
  507.0 2.2 all-to-all-done.6.second_ref
  510.2 9.9 %scatter_points.3 = f32[144,96,512]{2,1,0:T(8,128)} custom-call(s32[193]{0:T(256)} %copy-done.12, f32[144,96,512]{2,1,0:T(8,128)} %scatter_points.2.field_ref, bf16[192,16,256]{2,1,0:T(8,128)(2,1)} %broadcast_in_dim.44.dest_ref, bf16[8,144,2048]{2,1,0:T(8,128)(2,1)} %all-to-all-done.4.first_ref, ...), custom_call_target="tpu_custom_call", output_to_operand_aliasing={{}: (1, {})} | custom-call | flops 805306368 | bytes 15728640 | tf_op jit(solution)/shard_map/scatter_points/pallas_call | solution.py:321
  (70 shorter events, 17.2 us)
Async XLA Ops:
  0.0 6.6 %copy-start.11 = (s32[96,512]{1,0:T(8,128)S(1)}, s32[96,512]{1,0:T(8,128)}, u32[]{:S(2)}) copy-start(s32[96,512]{1,0:T(8,128)} %param.12) | copy-start | bytes 589828
  0.0 10.3 %copy-start.15 = (s32[4]{0:T(128)S(1)}, s32[4]{0:T(128)}, u32[]{:S(2)}) copy-start(s32[4]{0:T(128)} %steps_ref.5) | copy-start | bytes 52
  2.2 8.8 %collective-permute-start.1 = (f32[33,4,512]{2,1,0:T(4,128)S(1)}, f32[33,4,512]{2,1,0:T(4,128)S(1)}, u32[]{:S(2)}, u32[]{:S(2)}) collective-permute-start(f32[33,4,512]{2,1,0:T(4,128)S(1)} %pad_maximum_fusion.1), channel_id=1, source_target_pairs={{1,0},{2,1},{3,2},{5,4},{6,5},{7,6},{9,8},{10,9},{11,10},{13,12},{... | collective-permute-start | bytes 811016 | tf_op jit(solution)/shard_map/ppermute | solution.py:421
  3.5 7.4 %collective-permute-start = (f32[33,4,512]{2,1,0:T(4,128)S(1)}, f32[33,4,512]{2,1,0:T(4,128)S(1)}, u32[]{:S(2)}, u32[]{:S(2)}) collective-permute-start(f32[33,4,512]{2,1,0:T(4,128)S(1)} %pad_maximum_fusion), channel_id=1, source_target_pairs={{0,1},{1,2},{2,3},{4,5},{5,6},{6,7},{8,9},{9,10},{10,11},{12,13},{... | collective-permute-start | bytes 811016 | tf_op jit(solution)/shard_map/ppermute | solution.py:421
  10.2 1.2 copy-start.12
  10.9 0.7 copy-start.9
  10.9 0.8 copy-start.10
  11.7 1.0 copy-start
  46.6 55.0 %all-to-all-start = ((bf16[8,32,4096]{2,1,0:T(8,128)(2,1)}), bf16[8,32,4096]{2,1,0:T(8,128)(2,1)S(1)}, u32[]{:S(2)}, u32[]{:S(2)}) async-start(bf16[8,32,4096]{2,1,0:T(8,128)(2,1)} %gather_points.3.refs_1_), calls=%async_computation | async-start | bytes 4194304 | tf_op jit(solution)/shard_map/all_to_all | solution.py:492
  53.5 4.7 collective-permute-start.3
  54.8 4.7 collective-permute-start.2
  58.2 1.3 copy-start.7
  59.5 0.7 copy-start.8
  101.6 1.3 copy-start.3
  102.9 72.6 %all-to-all-start.1 = ((bf16[8,48,4096]{2,1,0:T(8,128)(2,1)}), bf16[8,48,4096]{2,1,0:T(8,128)(2,1)S(1)}, u32[]{:S(2)}, u32[]{:S(2)}) async-start(bf16[8,48,4096]{2,1,0:T(8,128)(2,1)} %gather_points.4.refs_1_), calls=%async_computation.1 | async-start | bytes 6291456 | tf_op jit(solution)/shard_map/all_to_all | solution.py:492
  108.4 8.4 %collective-permute-start.5 = (f32[64,4,512]{2,1,0:T(4,128)S(1)}, f32[64,4,512]{2,1,0:T(4,128)S(1)}, u32[]{:S(2)}, u32[]{:S(2)}) collective-permute-start(f32[64,4,512]{2,1,0:T(4,128)S(1)} %get-tuple-element.28), channel_id=1, source_target_pairs={{1,0},{2,1},{3,2},{5,4},{6,5},{7,6},{9,8},{10,9},{11,10},{13,12},{... | collective-permute-start | bytes 1572872 | tf_op jit(solution)/shard_map/ppermute | solution.py:421
  109.7 8.4 %collective-permute-start.4 = (f32[64,4,512]{2,1,0:T(4,128)S(1)}, f32[64,4,512]{2,1,0:T(4,128)S(1)}, u32[]{:S(2)}, u32[]{:S(2)}) collective-permute-start(f32[64,4,512]{2,1,0:T(4,128)S(1)} %get-tuple-element.27), channel_id=1, source_target_pairs={{0,1},{1,2},{2,3},{4,5},{5,6},{6,7},{8,9},{9,10},{10,11},{12,13},{... | collective-permute-start | bytes 1572872 | tf_op jit(solution)/shard_map/ppermute | solution.py:421
  116.8 1.3 copy-start.5
  118.1 0.8 copy-start.6
  175.6 56.4 %copy-start.2 = (bf16[8,48,4096]{2,1,0:T(8,128)(2,1)}, bf16[8,48,4096]{2,1,0:T(8,128)(2,1)S(1)}, u32[]{:S(2)}) copy-start(bf16[8,48,4096]{2,1,0:T(8,128)(2,1)S(1)} %all-to-all-done.1) | copy-start | bytes 9437188
  231.9 6.2 %copy-start.13 = (f32[32,36]{1,0:T(8,128)S(1)}, f32[32,36]{1,0:T(8,128)}, u32[]{:S(2)}) copy-start(f32[32,36]{1,0:T(8,128)} %param.16) | copy-start | bytes 13828
  231.9 7.3 %copy-start.14 = (f32[32,36]{1,0:T(8,128)S(1)}, f32[32,36]{1,0:T(8,128)}, u32[]{:S(2)}) copy-start(f32[32,36]{1,0:T(8,128)} %param.17) | copy-start | bytes 13828
  231.9 52.4 %all-to-all-start.3 = ((bf16[8,64,2048]{2,1,0:T(8,128)(2,1)}), bf16[8,64,2048]{2,1,0:T(8,128)(2,1)S(1)}, u32[]{:S(2)}, u32[]{:S(2)}) async-start(bf16[8,64,2048]{2,1,0:T(8,128)(2,1)} %get-tuple-element.36), calls=%async_computation.3 | async-start | bytes 4194304 | tf_op jit(solution)/shard_map/all_to_all | solution.py:492
  284.3 1.3 copy-start.4
  285.6 108.6 %all-to-all-start.4 = ((bf16[8,144,2048]{2,1,0:T(8,128)(2,1)}), bf16[8,144,2048]{2,1,0:T(8,128)(2,1)}, u32[]{:S(2)}, u32[]{:S(2)}) async-start(bf16[8,144,2048]{2,1,0:T(8,128)(2,1)} %bitcast.43), calls=%async_computation.4 | async-start | bytes 9437184 | tf_op jit(solution)/shard_map/all_to_all | solution.py:492
  480.2 28.9 %all-to-all-start.6 = ((bf16[8,32,2048]{2,1,0:T(8,128)(2,1)}), bf16[8,32,2048]{2,1,0:T(8,128)(2,1)S(1)}, u32[]{:S(2)}, u32[]{:S(2)}) async-start(bf16[8,32,2048]{2,1,0:T(8,128)(2,1)} %bitcast.21), calls=%async_computation.6 | async-start | bytes 2097152 | tf_op jit(solution)/shard_map/all_to_all | solution.py:492
  509.1 1.0 copy-start.1
